TPU v7x, 256 devices: a whole 4x4x8 slice. The times are simulated.
256 devices in a mesh: lead: 16 (over x, z_lo), space: 16 (over z_hi, y, core).
Axes of the slice: x: 4, y: 4, z: 8 (z_hi: 2, z_lo: 4; z = z_hi * 4 + z_lo), core: 2. Of those that a mesh axis runs over, the one named last changes fastest.
Arguments:
- latents: bfloat16 [16, 64, 128, 1024], P('lead', 'space'), may hold values from -6 to 6
- owners: int32 [2], replicated, may hold values from 0 to 15, as said below
- lead_ids: int32 [16], P('lead'), may hold values from 0 to 359
- film_scale: float32 [360, 1024], replicated, may hold values from -3 to 3
- film_shift: float32 [360, 1024], replicated, may hold values from -3 to 3
- w_qkv_row: bfloat16 [1024, 3072], P('space'), may hold values from -0.1875 to 0.1875
- w_out_row: bfloat16 [1024, 1024], P('space'), may hold values from -0.1875 to 0.1875
- gain_col: float32 [1024], replicated, may hold values from 0.25 to 1.75
- w_qkv_col: bfloat16 [1024, 3072], P('space'), may hold values from -0.1875 to 0.1875
- w_out_col: bfloat16 [1024, 1024], P('space'), may hold values from -0.1875 to 0.1875
Outputs:
- result: bfloat16 [16, 64, 128, 1024], P('lead', None, 'space')
Inputs may be any that keep to these rules, and one draw needn't show every extreme that they name: `owners`: the two analysis times are held by two different lead groups, one of which is the last lead group.
All inputs are finite; a program needn't handle non-finite values.
Results may differ from a plain program's by a relative error of at most 0.013.
Values may be sent and summed in bfloat16 or wider, within the bound.
A program may use at most 64 MiB of HBM per device.

v0:
```python
import jax
import jax.numpy as jnp
from jax import lax
from jax.sharding import PartitionSpec as P

HEADS = 8


def broadcast(shard, axis, root):
    mine = lax.axis_index(axis) == root
    return lax.psum(jnp.where(mine, shard, jnp.zeros_like(shard)), axis)


def rms_norm(values):
    return values * lax.rsqrt(jnp.mean(values * values, axis=-1, keepdims=True) + 1e-06)


def add_rows(left, piece):
    return jnp.dot(left, piece, preferred_element_type=jnp.float32)


def attend(tokens, w_qkv, w_out, score_form, mix_form):
    first_dim, second_dim, channels = tokens.shape
    head_dim = channels // HEADS
    flat_tokens = tokens.reshape(-1, channels)
    projected = add_rows(flat_tokens, lax.all_gather(w_qkv, "space", axis=0, tiled=True))
    projected = projected.astype(jnp.bfloat16).reshape(first_dim, second_dim, 3, HEADS, head_dim)
    queries = projected[:, :, 0]
    key_heads = projected[:, :, 1]
    values = projected[:, :, 2]
    scores = jnp.einsum(
        score_form, queries, key_heads, preferred_element_type=jnp.float32
    ) / jnp.sqrt(jnp.float32(head_dim))
    weights_soft = jax.nn.softmax(scores, axis=-1).astype(jnp.bfloat16)
    mixed = jnp.einsum(mix_form, weights_soft, values, preferred_element_type=jnp.float32).astype(
        jnp.bfloat16
    )
    mixed = mixed.reshape(-1, channels)
    outcome = add_rows(mixed, lax.all_gather(w_out, "space", axis=0, tiled=True))
    return outcome.reshape(first_dim, second_dim, channels)


def fetch_owner(slab, root):
    return broadcast(slab, "lead", root)


def on_device(
    latents,
    owners,
    lead_ids,
    film_scale,
    film_shift,
    w_qkv_row,
    w_out_row,
    gain_col,
    w_qkv_col,
    w_out_col,
):
    slab = latents[0]
    first_time = fetch_owner(slab, owners[0])
    second_time = fetch_owner(slab, owners[1])
    summed = first_time.astype(jnp.float32) + second_time.astype(jnp.float32)
    selector = (jnp.arange(film_scale.shape[0], dtype=jnp.int32) == lead_ids[0]).astype(
        jnp.float32
    )[None, :]
    film_gain = jnp.dot(selector, film_scale, precision=lax.Precision.HIGHEST)[0]
    film_bias = jnp.dot(selector, film_shift, precision=lax.Precision.HIGHEST)[0]
    hidden = (rms_norm(summed) * (1.0 + film_gain) + film_bias).astype(jnp.bfloat16)
    row_out = attend(hidden, w_qkv_row, w_out_row, "rihd,rjhd->rhij", "rhij,rjhd->rihd")
    after_rows = (hidden.astype(jnp.float32) + row_out).astype(jnp.bfloat16)
    columns = lax.all_to_all(after_rows, "space", split_axis=1, concat_axis=0, tiled=True)
    normed = (rms_norm(columns.astype(jnp.float32)) * gain_col).astype(jnp.bfloat16)
    column_out = attend(normed, w_qkv_col, w_out_col, "iwhd,jwhd->whij", "whij,jwhd->iwhd")
    result = (columns.astype(jnp.float32) + column_out).astype(jnp.bfloat16)
    return result[None]


def solution(mesh):
    placed = (
        P("lead", "space", None, None),
        P(),
        P("lead"),
        P(),
        P(),
        P("space", None),
        P("space", None),
        P(),
        P("space", None),
        P("space", None),
    )
    return jax.shard_map(
        on_device,
        mesh=mesh,
        in_specs=placed,
        out_specs=P("lead", None, "space", None),
        check_vma=False,
    )
```

profile of v0, /device:TPU:1, one launch (start us, length us, event | category | flops | bytes accessed | tf_op | source)
XLA Modules:
  0.0 399.4 jit_solution(1498395616614010390)
XLA Ops:
  7.4 1.4 fusion.46
  10.1 2.7 select_bitcast_fusion.1
  16.4 249.7 %all-reduce.3.cloned.1.call-done = (bf16[4,128,1024]{2,1,0:T(8,128)(2,1)}, bf16[4,128,1024]{2,1,0:T(8,128)(2,1)}) async-done(((bf16[4,128,1024]{2,1,0:T(8,128)(2,1)}, bf16[4,128,1024]{2,1,0:T(8,128)(2,1)}), (bf16[4,128,1024]{2,1,0:T(8,128)(2,1)}, bf16[4,128,1024]{2,1,0:T(8,128)(2,1)})) %all-reduce.3.cloned.1.call-update) | async-done | bytes 2097168 | tf_op jit(solution)/shard_map/psum | solution.py:11
  266.1 2.1 multiply_reduce_fusion
  268.8 6.4 %fusion.10 = bf16[64,8,24,128]{3,1,2,0:T(8,128)(2,1)S(1)} fusion(bf16[512,1024]{1,0:T(8,128)(2,1)S(1)} %bitcast.107, bf16[1024,3072]{1,0:T(8,128)(2,1)} %all-gather.5.cloned.1.call-done), kind=kOutput, calls=%fused_computation.24 | convolution fusion | flops 3222798336 | bytes 10485760 | tf_op jit(solution)/shard_map/dot_general | solution.py:19
  276.1 2.0 fusion.45
  278.1 2.4 copy.63
  280.4 2.5 fusion.47
  283.0 3.7 fusion.22
  286.7 3.8 convolution_convert_fusion.3
  290.5 3.2 add_convert_fusion
  293.7 1.8 copy.50
  295.5 20.8 %all-to-all-start = ((bf16[4,128,1024]{2,0,1:T(4,128)(2,1)}), bf16[4,128,1024]{2,0,1:T(4,128)(2,1)S(1)}, u32[]{:S(2)}, u32[]{:S(2)}) async-start(bf16[4,128,1024]{2,0,1:T(4,128)(2,1)} %copy.50), calls=%async_computation | async-start | bytes 2097152 | tf_op jit(solution)/shard_map/all_to_all | solution.py:71
  317.0 27.3 %all-to-all-done = bf16[4,128,1024]{2,0,1:T(4,128)(2,1)S(1)} async-done(((bf16[4,128,1024]{2,0,1:T(4,128)(2,1)}), bf16[4,128,1024]{2,0,1:T(4,128)(2,1)S(1)}, u32[]{:S(2)}, u32[]{:S(2)}) %all-to-all-start) | async-done | bytes 1048608 | tf_op jit(solution)/shard_map/all_to_all | solution.py:71
  344.7 1.5 copy.52
  346.9 1.8 fusion.6
  348.7 6.6 %convolution_convert_fusion = bf16[512,3072]{1,0:T(8,128)(2,1)S(1)} fusion(bf16[512,1024]{1,0:T(8,128)(2,1)S(1)} %fusion.6, bf16[1024,3072]{1,0:T(8,128)(2,1)} %all-gather.9.cloned.1.call-done), kind=kOutput, calls=%fused_computation.2 | convolution fusion | flops 3222798336 | bytes 10485760 | tf_op jit(solution)/shard_map/dot_general | solution.py:19
  355.3 2.2 fusion.44
  357.6 3.9 fusion.48
  361.5 4.9 %fusion.21 = f32[8,8,64,64]{2,3,1,0:T(8,128)} fusion(bf16[64,8,1,8,128]{4,1,3,2,0:T(8,128)(2,1)} %get-tuple-element.9, bf16[64,8,1,8,128]{4,1,3,2,0:T(8,128)(2,1)S(1)} %get-tuple-element.7), kind=kOutput, calls=%fused_computation.34 | convolution fusion | flops 67108864 | bytes 3145728 | tf_op jit(solution)/shard_map/iwhd,jwhd->whij/dot_general | solution.py:31
  366.4 4.8 %fusion.17 = bf16[64,8,8,128]{3,0,2,1:T(8,128)(2,1)} fusion(bf16[64,8,1,8,128]{4,1,3,2,0:T(8,128)(2,1)} %get-tuple-element.8, f32[8,8,64]{2,1,0:T(8,128)S(1)} %fusion.48, f32[8,8,64,64]{2,3,1,0:T(8,128)} %fusion.21), kind=kOutput, calls=%fused_computation.31 | convolution fusion | flops 68685888 | bytes 3162112 | tf_op jit(solution)/shard_map/whij,jwhd->iwhd/dot_general | solution.py:35
  371.2 1.9 copy.59
  374.3 12.7 %all-gather.11.cloned.1.call-done = bf16[1024,1024]{1,0:T(8,128)(2,1)} async-done(((bf16[64,1024]{1,0:T(8,128)(2,1)}), bf16[1024,1024]{1,0:T(8,128)(2,1)}) %all-gather.11.cloned.1.call-update) | async-done | bytes 2097168 | tf_op jit(solution)/shard_map/all_gather | solution.py:39
  387.1 4.8 %fusion.18 = bf16[1,64,8,1024]{3,2,1,0:T(8,128)(2,1)} fusion(bf16[64,8,1024]{2,1,0:T(8,128)(2,1)} %dot_general.44, bf16[1024,1024]{1,0:T(8,128)(2,1)} %all-gather.11.cloned.1.call-done, f32[16,4,8,1024]{3,2,1,0:T(8,128)} %copy.52), kind=kOutput, calls=%fused_computation.32 | convolution fusion | flops 1074790400 | bytes 6291456 | tf_op jit(solution)/shard_map/dot_general | solution.py:19
  (38 shorter events, 7.3 us)
Async XLA Ops:
  7.4 7.8 %copy-start = (f32[360,1024]{1,0:T(8,128)S(1)}, f32[360,1024]{1,0:T(8,128)}, u32[]{:S(2)}) copy-start(f32[360,1024]{1,0:T(8,128)} %param.13) | copy-start | bytes 4423684
  7.4 258.7 %all-reduce.3.cloned.1.call-start = ((), (), s32[]{:S(2)}) async-start(), calls=%async_computation.5 | async-start | bytes 4194304 | tf_op jit(solution)/shard_map/psum | solution.py:11
  12.7 3.1 copy-start.3
  12.8 256.0 %all-gather.5.cloned.1.call-start = ((), (), s32[]{:S(2)}) async-start(), calls=%async_computation.1 | async-start | bytes 6684672 | tf_op jit(solution)/shard_map/all_gather | solution.py:26
  13.4 277.1 %all-gather.7.cloned.1.call-start = ((), (), s32[]{:S(2)}) async-start(), calls=%async_computation.2 | async-start | bytes 2228224 | tf_op jit(solution)/shard_map/all_gather | solution.py:39
  13.9 334.8 %all-gather.9.cloned.1.call-start = ((), (), s32[]{:S(2)}) async-start(), calls=%async_computation.3 | async-start | bytes 6684672 | tf_op jit(solution)/shard_map/all_gather | solution.py:26
  266.1 2.1 copy-start.1
  266.1 2.2 copy-start.2
  295.5 48.9 %all-to-all-start = ((bf16[4,128,1024]{2,0,1:T(4,128)(2,1)}), bf16[4,128,1024]{2,0,1:T(4,128)(2,1)S(1)}, u32[]{:S(2)}, u32[]{:S(2)}) async-start(bf16[4,128,1024]{2,0,1:T(4,128)(2,1)} %copy.50), calls=%async_computation | async-start | bytes 2097152 | tf_op jit(solution)/shard_map/all_to_all | solution.py:71
  316.3 70.8 %all-gather.11.cloned.1.call-start = ((), (), s32[]{:S(2)}) async-start(), calls=%async_computation.4 | async-start | bytes 2228224 | tf_op jit(solution)/shard_map/all_gather | solution.py:39
  344.7 2.1 copy-start.4
Sparse Core Ops, SparseCore 0:
  12.9 253.1 all-reduce.2
Sparse Core Ops, SparseCore 1:
  16.0 95.7 all-gather.4
  114.4 63.3 all-gather.6
  180.3 76.8 all-gather.8
  319.8 67.2 all-gather.10
where the time goes:
time: 400 us; the launch traced here: 399 us
  waiting for transfers between devices  292 us (73%)
  matrix products  45.8 us (11%)
  starting transfers between devices  21 us (5%)
  between operations  17.1 us (4%)
  local copies, waits for them, and re-layouts  15.6 us (4%)
  other arithmetic  7.85 us (2%)
    psum x1, waiting for transfers between devices, broadcast(): return lax.psum(jnp.where(mine, shard, jnp.zeros_like(shard)), axis)  250 us
    all_to_all x1, waiting for transfers between devices, on_device(): lax.all_to_all(after_rows, 'space', split_axis=1, concat_axis=0, tiled=True)  27.3 us
    dot_general x4, matrix products, add_rows(): return jnp.dot(left, piece, preferred_element_type=jnp.float32)  21 us
    all_to_all x1, starting transfers between devices, on_device(): lax.all_to_all(after_rows, 'space', split_axis=1, concat_axis=0, tiled=True)  20.8 us
    all_gather x2, waiting for transfers between devices, attend(): lax.all_gather(w_out, 'space', axis=0, tiled=True)  12.7 us
    dot_general x2, matrix products, attend(): jnp.einsum(score_form, queries, key_heads, preferred_element_type=jnp.flo...  8.63 us
    dot_general x2, matrix products, attend(): jnp.einsum(mix_form, weights_soft, values, preferred_element_type=jnp.flo...  8.57 us
  transfers between devices with their start and end apart: 6, of which 3 were waited for; matrix products, arithmetic and copies ran while one was open for 15% of the time, Pallas kernels for 0%

commit v1 on v0

v1 whole, which is shorter than its diff:
```python
import functools

import jax
import jax.numpy as jnp
from jax import lax
from jax.experimental import pallas as pl
from jax.experimental.pallas import tpu as pltpu
from jax.sharding import PartitionSpec as P

HEADS = 8
DIM = 128
C = 1024
MESH = pl.DeviceIdType.MESH
BF = jnp.bfloat16
F32 = jnp.float32
TILE = 256
SENDS = 160


def softmax_rows(scores):
    top = jnp.max(scores, axis=-1, keepdims=True)
    weights = jnp.exp((scores - top) * (DIM**-0.5))
    return weights / jnp.sum(weights, axis=-1, keepdims=True)


def kernel(
    slab_in, owners, lead_ids, scale_in, shift_in, wqr_in, wor_in, gain, wqc_in, woc_in,
    out,
    slab, scale_t, shift_t, rx, sx, rz, nb, hid, kv, qb, mixed, send, cols, xf,
    wqr, wor, wqc, woc,
    ssem, loc, s_rx, s_rz, s_ax, s_az, s_wz, s_wy, s_wx, s_wd, s_a2a,
):
    lead = lax.axis_index("lead")
    space = lax.axis_index("space")
    x, zl = lead // 4, lead % 4
    h, y, c = space // 8, (space // 2) % 4, space % 2
    z = h * 4 + zl
    p = x % 2
    yc = space % 8

    def at(x=x, y=y, z=z, c=c):
        return ((x % 4) * 4 + z % 4, (z // 4) * 8 + (y % 4) * 2 + c)

    def zmod(v):
        return (v + 8) % 8

    started = []

    def push(src, dst, recv, dev):
        copy = pltpu.make_async_remote_copy(
            src, dst, ssem.at[len(started)], recv, device_id=dev, device_id_type=MESH
        )
        copy.start()
        started.append(copy)

    def arrived(dst, recv):
        pltpu.make_async_remote_copy(
            dst, dst, ssem.at[0], recv, device_id=at(c=1 - c), device_id_type=MESH
        ).wait_recv()

    weights_in = ((wqr_in, wor_in), (wqc_in, woc_in))
    weights = ((wqr, wor), (wqc, woc))

    local = []

    def pull(src, dst):
        copy = pltpu.make_async_copy(src, dst, loc.at[len(local)])
        copy.start()
        local.append(copy)
        return copy

    slab_copy = pull(slab_in, slab)
    half = pl.ds(pl.multiple_of(p * 32, 32), 32)
    other_half = pl.ds(pl.multiple_of((1 - p) * 32, 32), 32)
    own_copies = [
        [pull(weights_in[a][j].at[half], weights[a][j].at[h, y, c, half]) for j in range(2)]
        for a in range(2)
    ]
    table_copies = [pull(scale_in, scale_t), pull(shift_in, shift_t)]

    barrier = pltpu.get_barrier_semaphore()
    peers = [at(x=x + d) for d in range(1, 4)]
    peers += [at(z=zmod(z + d)) for d in range(1, 8)]
    peers += [at(y=y + d, c=e) for d in range(1, 4) for e in range(2)]
    peers += [at(c=1 - c)]
    for peer in peers:
        pl.semaphore_signal(barrier, 1, device_id=peer, device_id_type=MESH)
    pl.semaphore_wait(barrier, len(peers))

    def weights_z(a):
        for j in range(2):
            push(weights_in[a][j].at[half], weights[a][j].at[h, y, c, half], s_wz.at[a, j], at(z=7 - z))

    def weights_z_arrived(a):
        for j in range(2):
            arrived(weights[a][j].at[1 - h, y, c, half], s_wz.at[a, j])

    def weights_y(a, k):
        for j in range(2):
            hh = h if k == 0 else 1 - h
            block = weights[a][j].at[hh, y, c, half]
            src = weights_in[a][j].at[half] if k == 0 else block
            for d in (1, 3, 2):
                push(src, block, s_wy.at[a, j, k, d - 1], at(y=y + d))

    def weights_x(a, k):
        hh = h if k == 0 else 1 - h
        for j in range(2):
            if k == 0:
                own_copies[a][j].wait()
            for d in (1, 3, 2):
                arrived(weights[a][j].at[hh, (y + 4 - d) % 4, c, half], s_wy.at[a, j, k, d - 1])
            for e in range(2):
                rows = pl.ds(pl.multiple_of(p * 32 + e * 16, 16), 16)
                block = weights[a][j].at[hh, :, c, rows]
                push(block, block, s_wx.at[a, j, k, e], at(x=x + (1 if e == 0 else 3)))
            block = weights[a][j].at[hh, :, c, half]
            push(block, block, s_wd.at[a, j, k, 0], at(c=1 - c))

    def weights_d(a, k):
        hh = h if k == 0 else 1 - h
        for j in range(2):
            for e in range(2):
                rows = pl.ds(pl.multiple_of((1 - p) * 32 + e * 16, 16), 16)
                arrived(weights[a][j].at[hh, :, c, rows], s_wx.at[a, j, k, e])
            block = weights[a][j].at[hh, :, c, other_half]
            push(block, block, s_wd.at[a, j, k, 1], at(c=1 - c))

    def weights_ready(a, j):
        for k in range(2):
            hh = h if k == 0 else 1 - h
            arrived(weights[a][j].at[hh, :, 1 - c, half], s_wd.at[a, j, k, 0])
            arrived(weights[a][j].at[hh, :, 1 - c, other_half], s_wd.at[a, j, k, 1])

    weights_z(0)
    slab_copy.wait()
    mine = jnp.logical_or(owners[0] == lead, owners[1] == lead)
    keep = jnp.where(mine, 1.0, 0.0).astype(F32)

    @pl.loop(0, 8)
    def _(i):
        rows = pl.ds(pl.multiple_of(i * 64, 64), 64)
        slab[rows, :] = (slab[rows, :].astype(F32) * keep).astype(BF)

    for d in (1, 3, 2):
        xt = (x + d) % 4
        push(slab.at[pl.ds(pl.multiple_of(xt * 128, 128), 128)], rx.at[d - 1], s_rx.at[d - 1], at(x=xt))
    weights_y(0, 0)
    for d in (1, 3, 2):
        arrived(rx.at[d - 1], s_rx.at[d - 1])

    @pl.loop(0, 4)
    def _(i):
        rows = pl.ds(pl.multiple_of(i * 32, 32), 32)
        own = slab[pl.ds(pl.multiple_of(x * 128 + i * 32, 32), 32), :].astype(F32)
        total = own + rx[0, rows, :].astype(F32) + rx[1, rows, :].astype(F32) + rx[2, rows, :].astype(F32)
        sx[rows, :] = total.astype(BF)

    for d in (1, 3, 2):
        zt = (zl + d) % 4
        push(sx.at[pl.ds(pl.multiple_of(zt * 32, 32), 32)], rz.at[d - 1], s_rz.at[d - 1], at(z=h * 4 + zt))
    weights_z_arrived(0)
    weights_y(0, 1)
    for d in (1, 3, 2):
        arrived(rz.at[d - 1], s_rz.at[d - 1])
    total = sx[pl.ds(pl.multiple_of(zl * 32, 32), 32), :].astype(F32)
    total = total + rz[0].astype(F32) + rz[1].astype(F32) + rz[2].astype(F32)
    total = total * lax.rsqrt(jnp.mean(total * total, axis=-1, keepdims=True) + 1e-06)
    nb[h, x, zl] = total.astype(BF)

    for d in (1, 3, 2):
        piece = nb.at[h, x, zl]
        push(piece, piece, s_ax.at[d - 1], at(x=x + d))
    for d in (1, 3, 2):
        arrived(nb.at[h, (x + 4 - d) % 4, zl], s_ax.at[d - 1])

    def ring_rows(t, way):
        return slice(0, 4) if t < 4 else (slice(0, 2) if way == 0 else slice(2, 4))

    def ring_send(t):
        for way in range(2):
            source = zmod(z - (t - 1)) if way == 0 else zmod(z + (t - 1))
            target = zmod(z + 1) if way == 0 else zmod(z - 1)
            rows = ring_rows(t, way)
            piece = nb.at[source // 4, pl.ds(rows.start, rows.stop - rows.start), source % 4]
            push(piece, piece, s_az.at[t - 1, way], at(z=target))

    def ring_arrived(t):
        for way in range(2):
            source = zmod(z - t) if way == 0 else zmod(z + t)
            rows = ring_rows(t, way)
            arrived(
                nb.at[source // 4, pl.ds(rows.start, rows.stop - rows.start), source % 4],
                s_az.at[t - 1, way],
            )

    ring_send(1)
    weights_x(0, 0)
    ring_arrived(1)
    ring_send(2)
    weights_x(0, 1)
    weights_z(1)
    weights_y(1, 0)
    ring_arrived(2)
    ring_send(3)
    weights_d(0, 0)
    ring_arrived(3)
    ring_send(4)
    weights_d(0, 1)
    weights_z_arrived(1)
    weights_y(1, 1)
    for copy in table_copies:
        copy.wait()
    time = lead_ids[0]
    film_gain = 1.0 + scale_t[pl.ds(time, 1), :]
    film_bias = shift_t[pl.ds(time, 1), :]
    ring_arrived(4)
    weights_ready(0, 0)

    def row_step(hp):
        @pl.loop(0, 8)
        def _(i):
            part = nb[hp, i // 2, pl.ds((i % 2) * 2, 2)].reshape(64, C)
            rows = pl.ds(pl.multiple_of(i * 64, 64), 64)
            hid[rows, :] = (part.astype(F32) * film_gain + film_bias).astype(BF)

        @pl.loop(0, 8)
        def _(t):
            block = wqr[:, :, :, :, pl.ds(pl.multiple_of(C + t * TILE, TILE), TILE)].reshape(C, TILE)
            cut = pl.ds(pl.multiple_of(t * TILE, TILE), TILE)
            kv[:, cut] = jnp.dot(hid[...], block, preferred_element_type=F32).astype(BF)

        here = pl.ds(pl.multiple_of(h * 64, 64), 64)

        def wanted(cols_cut):
            return jnp.concatenate(
                [hid[pl.ds(pl.multiple_of(r * 128 + h * 64, 64), 64), cols_cut] for r in range(4)], axis=0
            )

        @pl.loop(0, 4)
        def _(t):
            cut = pl.ds(pl.multiple_of(t * TILE, TILE), TILE)
            block = wqr[:, :, :, :, cut].reshape(C, TILE)
            qb[:, cut] = jnp.dot(wanted(slice(None)), block, preferred_element_type=F32).astype(BF)

        for head in range(HEADS):
            cut = slice(head * DIM, (head + 1) * DIM)
            vcut = slice(C + head * DIM, C + (head + 1) * DIM)
            q = qb[:, cut].reshape(4, 64, DIM)
            keys = kv[:, cut].reshape(4, 128, DIM)
            values = kv[:, vcut].reshape(4, 128, DIM)
            scores = lax.dot_general(q, keys, (((2,), (2,)), ((0,), (0,))), preferred_element_type=F32)
            probs = softmax_rows(scores).astype(BF)
            mix = lax.dot_general(probs, values, (((2,), (1,)), ((0,), (0,))), preferred_element_type=F32)
            mixed[pl.ds(0, 256), cut] = mix.reshape(256, DIM).astype(BF)

        if hp == 0:
            weights_ready(0, 1)

        @pl.loop(0, 4)
        def _(t):
            cut = pl.ds(pl.multiple_of(t * TILE, TILE), TILE)
            block = wor[:, :, :, :, cut].reshape(C, TILE)
            grown = jnp.dot(mixed[pl.ds(0, 256), :], block, preferred_element_type=F32)
            grown = (grown + wanted(cut).astype(F32)).reshape(4, 64, TILE)
            for d in range(8):
                send[hp, d, :, cut] = grown[:, d * 8 : (d + 1) * 8, :].reshape(32, TILE).astype(BF)

        for dy in (2, 1, 3, 0):
            for dc in range(2):
                if dy == 0 and dc == 0:
                    continue
                ty, tc = (y + dy) % 4, (c + dc) % 2
                push(
                    send.at[hp, ty * 2 + tc], cols.at[hp, yc], s_a2a.at[hp, dy * 2 + dc], at(y=ty, c=tc)
                )
        return pull(send.at[hp, yc], cols.at[hp, yc])

    def row_arrived(hp):
        for dy in (2, 1, 3, 0):
            for dc in range(2):
                if dy == 0 and dc == 0:
                    continue
                sy, sc = (y + 4 - dy) % 4, (c + dc) % 2
                arrived(cols.at[hp, sy * 2 + sc], s_a2a.at[hp, dy * 2 + dc])

    own0 = row_step(0)
    weights_x(1, 0)
    own1 = row_step(1)
    weights_x(1, 1)
    weights_d(1, 0)
    weights_d(1, 1)
    own0.wait()
    own1.wait()
    row_arrived(0)
    row_arrived(1)

    for hp in range(2):
        @pl.loop(0, 8)
        def _(i):
            part = cols[hp, i].astype(F32)
            part = part * lax.rsqrt(jnp.mean(part * part, axis=-1, keepdims=True) + 1e-06) * gain[...]
            rows = pl.ds(pl.multiple_of(hp * 256 + i * 32, 32), 32)
            for s in range(8):
                xf[s, rows, :] = part[:, s * DIM : (s + 1) * DIM]

    for w in range(8):
        for s in range(8):
            hid[w * 64 : (w + 1) * 64, s * DIM : (s + 1) * DIM] = xf[s, pl.ds(w, 64, stride=8), :].astype(BF)

    weights_ready(1, 0)

    @pl.loop(0, 8)
    def _(t):
        block = wqc[:, :, :, :, pl.ds(pl.multiple_of(C + t * TILE, TILE), TILE)].reshape(C, TILE)
        cut = pl.ds(pl.multiple_of(t * TILE, TILE), TILE)
        kv[:, cut] = jnp.dot(hid[...], block, preferred_element_type=F32).astype(BF)

    @pl.loop(0, 4)
    def _(t):
        cut = pl.ds(pl.multiple_of(t * TILE, TILE), TILE)
        block = wqc[:, :, :, :, cut].reshape(C, TILE)
        mixed[:, cut] = jnp.dot(hid[...], block, preferred_element_type=F32).astype(BF)

    for head in range(HEADS):
        cut = slice(head * DIM, (head + 1) * DIM)
        vcut = slice(C + head * DIM, C + (head + 1) * DIM)
        q = mixed[:, cut].reshape(8, 64, DIM)
        keys = kv[:, cut].reshape(8, 64, DIM)
        values = kv[:, vcut].reshape(8, 64, DIM)
        scores = lax.dot_general(q, keys, (((2,), (2,)), ((0,), (0,))), preferred_element_type=F32)
        probs = softmax_rows(scores).astype(BF)
        mix = lax.dot_general(probs, values, (((2,), (1,)), ((0,), (0,))), preferred_element_type=F32)
        for w in range(8):
            xf[head, pl.ds(w, 64, stride=8), :] = mix[w]
        hid[:, cut] = xf[head].astype(BF)

    weights_ready(1, 1)

    @pl.loop(0, 4)
    def _(t):
        cut = pl.ds(pl.multiple_of(t * TILE, TILE), TILE)
        block = woc[:, :, :, :, cut].reshape(C, TILE)
        grown = jnp.dot(hid[...], block, preferred_element_type=F32)
        out[:, cut] = (grown + cols[:, :, :, cut].reshape(512, TILE).astype(F32)).astype(BF)

    for copy in started:
        copy.wait_send()


def on_device(
    latents, owners, lead_ids, film_scale, film_shift, w_qkv_row, w_out_row, gain_col, w_qkv_col, w_out_col
):
    anywhere = pl.BlockSpec(memory_space=pl.ANY)
    scalars = pl.BlockSpec(memory_space=pltpu.SMEM)
    vector = pl.BlockSpec(memory_space=pltpu.VMEM)
    dma = pltpu.SemaphoreType.DMA
    result = pl.pallas_call(
        kernel,
        out_shape=jax.ShapeDtypeStruct((512, C), BF),
        in_specs=[
            anywhere, scalars, scalars, anywhere, anywhere, anywhere, anywhere, vector, anywhere, anywhere
        ],
        out_specs=vector,
        scratch_shapes=[
            pltpu.VMEM((512, C), BF),
            pltpu.VMEM((360, C), F32),
            pltpu.VMEM((360, C), F32),
            pltpu.VMEM((3, 128, C), BF),
            pltpu.VMEM((128, C), BF),
            pltpu.VMEM((3, 32, C), BF),
            pltpu.VMEM((2, 4, 4, 32, C), BF),
            pltpu.VMEM((512, C), BF),
            pltpu.VMEM((512, 2 * C), BF),
            pltpu.VMEM((256, C), BF),
            pltpu.VMEM((512, C), BF),
            pltpu.VMEM((2, 8, 32, C), BF),
            pltpu.VMEM((2, 8, 32, C), BF),
            pltpu.VMEM((8, 512, DIM), F32),
            pltpu.VMEM((2, 4, 2, 64, 3 * C), BF),
            pltpu.VMEM((2, 4, 2, 64, C), BF),
            pltpu.VMEM((2, 4, 2, 64, 3 * C), BF),
            pltpu.VMEM((2, 4, 2, 64, C), BF),
            dma((SENDS,)),
            dma((9,)),
            dma((3,)),
            dma((3,)),
            dma((3,)),
            dma((4, 2)),
            dma((2, 2)),
            dma((2, 2, 2, 3)),
            dma((2, 2, 2, 2)),
            dma((2, 2, 2, 2)),
            dma((2, 8)),
        ],
        compiler_params=pltpu.CompilerParams(
            collective_id=0, has_side_effects=True, vmem_limit_bytes=56 << 20
        ),
        name="axial_attention",
    )(
        latents.reshape(512, C), owners, lead_ids, film_scale, film_shift,
        w_qkv_row, w_out_row, gain_col.reshape(1, C), w_qkv_col, w_out_col,
    )
    return result.reshape(1, 64, 8, C)


def solution(mesh):
    placed = (
        P("lead", "space", None, None),
        P(),
        P("lead"),
        P(),
        P(),
        P("space", None),
        P("space", None),
        P(),
        P("space", None),
        P("space", None),
    )
    return jax.shard_map(
        on_device,
        mesh=mesh,
        in_specs=placed,
        out_specs=P("lead", None, "space", None),
        check_vma=False,
    )
```

time: 400 us -> 124 us (0.31)
  waiting for transfers between devices: 292 us -> 0 us
  Pallas kernels: 0 us -> 121 us
  matrix products: 45.8 us -> 0 us
  starting transfers between devices: 21 us -> 0 us
  between operations: 17.1 us -> 0.66 us
  local copies, waits for them, and re-layouts: 15.6 us -> 2.26 us
  other arithmetic: 7.85 us -> 0 us
    psum x1 -> x0, waiting for transfers between devices: 250 us -> none  [broadcast(): return lax.psum(jnp.where(mine, shard, jnp.zeros_like(shard)), axis)]
    pallas_call x0 -> x1, Pallas kernels: none -> 121 us  [on_device(): pl.pallas_call(kernel, out_shape=jax.ShapeDtypeStruct((512, C), BF), in_s...]
    dot_general x10 -> x0, matrix products: 39.4 us -> none  [the longest x4 21 us: add_rows(): return jnp.dot(left, piece, preferred_element_type=jnp.float32)]
    all_to_all x1 -> x0, waiting for transfers between devices: 27.3 us -> none  [on_device(): lax.all_to_all(after_rows, 'space', split_axis=1, concat_axis=0, tiled=True)]
    all_to_all x1 -> x0, starting transfers between devices: 20.8 us -> none  [on_device(): lax.all_to_all(after_rows, 'space', split_axis=1, concat_axis=0, tiled=True)]
    all_gather x4 -> x0, waiting for transfers between devices: 12.8 us -> none  [the longest x2 12.7 us: attend(): lax.all_gather(w_out, 'space', axis=0, tiled=True)]
    sub x2 -> x0, matrix products: 6.42 us -> none  [attend(): weights_soft = jax.nn.softmax(scores, axis=-1).astype(jnp.bfloat16)]
    slice x3 -> x0, local copies, waits for them, and re-layouts: 5.59 us -> none  [the longest x2 4.2 us: attend(): queries = projected[:, :, 0]]
  transfers between devices with their start and end apart: 6 -> 0, of which waited for: 3 -> 0; matrix products, arithmetic and copies ran while one was open for 15% -> 0% of each run, Pallas kernels for 0% -> 0%
where the time goes in v1:
time: 124 us
  Pallas kernels  121 us (98%)
  local copies, waits for them, and re-layouts  2.26 us (2%)
    pallas_call x1, Pallas kernels, on_device(): pl.pallas_call(kernel, out_shape=jax.ShapeDtypeStruct((512, C), BF), in_s...  121 us

profile of v1, /device:TPU:1, one launch (start us, length us, event | category | flops | bytes accessed | tf_op | source)
XLA Modules:
  0.0 123.8 jit_solution(16493356189406744568)
XLA Ops:
  0.7 120.9 %axial_attention.1 = bf16[512,1024]{1,0:T(8,128)(2,1)} custom-call(bf16[512,1024]{1,0:T(8,128)(2,1)} %bitcast.4, s32[2]{0:T(128)} %owners.1, s32[1]{0:T(128)S(6)} %copy.12.lead_ids, f32[360,1024]{1,0:T(8,128)} %scale_in.1, f32[360,1024]{1,0:T(8,128)} %shift_in.1, bf16[64,3072]{1,0:T(8,128)(2,1)} %wqr_in.1, bf16[64,1024]{1,0:T(8,128)(2,1)} %wor_in.1, ...), custom_call_target="tpu_custom_call" | custom-call | tf_op jit(solution)/shard_map/axial_attention/pallas_call | solution.py:358
  121.5 2.3 %copy.13 = bf16[1,64,8,1024]{3,2,1,0:T(8,128)(2,1)} copy(bf16[1,64,8,1024]{3,2,1,0:T(8,128)(2,1)} %bitcast.3) | data formatting | bytes 2097152

commit v2 on v1

v2 whole, which is shorter than its diff:
```python
import functools

import jax
import jax.numpy as jnp
from jax import lax
from jax.experimental import pallas as pl
from jax.experimental.pallas import tpu as pltpu
from jax.sharding import PartitionSpec as P

HEADS = 8
DIM = 128
C = 1024
MESH = pl.DeviceIdType.MESH
BF = jnp.bfloat16
F32 = jnp.float32
TILE = 1024
SENDS = 200


def softmax_rows(scores):
    top = jnp.max(scores, axis=-1, keepdims=True)
    weights = jnp.exp((scores - top) * (DIM**-0.5))
    return weights / jnp.sum(weights, axis=-1, keepdims=True)


def kernel(
    slab_in, owners, lead_ids, scale_in, shift_in, wqr_in, wor_in, gain, wqc_in, woc_in,
    out,
    slab, scale_t, shift_t, rx, sx, rz, nb, hid, kv, qb, mixed, send, cols, xf,
    wqr, wor, wqc, woc,
    ssem, loc, s_rx, s_rz, s_ax, s_az, s_edge, s_ny, s_wz, s_wy, s_wf, s_wx, s_wd, s_a2a,
):
    lead = lax.axis_index("lead")
    space = lax.axis_index("space")
    x, zl = lead // 4, lead % 4
    h, y, c = space // 8, (space // 2) % 4, space % 2
    z = h * 4 + zl
    p = x % 2
    yc = space % 8

    def at(x=x, y=y, z=z, c=c):
        return ((x % 4) * 4 + z % 4, (z // 4) * 8 + (y % 4) * 2 + c)

    def zmod(v):
        return (v + 8) % 8

    started = []

    def push(src, dst, recv, dev):
        copy = pltpu.make_async_remote_copy(
            src, dst, ssem.at[len(started)], recv, device_id=dev, device_id_type=MESH
        )
        copy.start()
        started.append(copy)

    def arrived(dst, recv):
        pltpu.make_async_remote_copy(
            dst, dst, ssem.at[0], recv, device_id=at(c=1 - c), device_id_type=MESH
        ).wait_recv()

    weights_in = ((wqr_in, wor_in), (wqc_in, woc_in))
    weights = ((wqr, wor), (wqc, woc))

    local = []

    def pull(src, dst):
        copy = pltpu.make_async_copy(src, dst, loc.at[len(local)])
        copy.start()
        local.append(copy)
        return copy

    slab_copy = pull(slab_in, slab)
    half = pl.ds(pl.multiple_of(p * 32, 32), 32)
    other_half = pl.ds(pl.multiple_of((1 - p) * 32, 32), 32)
    own_copies = [
        [pull(weights_in[0][j].at[half], weights[0][j].at[h, y, c, half]) for j in range(2)],
        [pull(weights_in[1][j], weights[1][j].at[h, y, c]) for j in range(2)],
    ]
    table_copies = [pull(scale_in, scale_t), pull(shift_in, shift_t)]

    barrier = pltpu.get_barrier_semaphore()
    peers = [at(x=x + d) for d in range(1, 4)]
    peers += [at(y=y + d) for d in range(1, 4)]
    peers += [at(z=h * 4 + (zl + d) % 4) for d in range(1, 4)]
    peers += [at(z=7 - z), at(c=1 - c)]
    for peer in peers:
        pl.semaphore_signal(barrier, 1, device_id=peer, device_id_type=MESH)
    pl.semaphore_wait(barrier, len(peers))

    def side(k):
        return h if k == 0 else 1 - h

    edge = jnp.logical_or(zl == 0, zl == 3)
    inner = h * 4 + jnp.where(zl == 0, 1, 2)

    def edge_copy(a, j, forward):
        own = weights_in[a][j].at[half]
        there = weights[a][j].at[h, y, c, half]
        far = weights[a][j].at[1 - h, y, c, half]
        return pltpu.make_async_remote_copy(
            far if forward else own,
            far if forward else there,
            s_edge.at[a, j, int(forward)],
            s_wz.at[a, j],
            device_id=at(z=inner if forward else 7 - z),
            device_id_type=MESH,
        )

    def far_z(a, j):
        @pl.when(edge)
        def _():
            edge_copy(a, j, False).start()

    def far_y(a, j, k):
        block = weights[a][j].at[side(k), y, c, half]
        if k == 1:
            arrived(block, s_wz.at[a, j])

            @pl.when(edge)
            def _():
                edge_copy(a, j, True).start()

        src = weights_in[a][j].at[half] if k == 0 else block
        for d in (1, 3):
            push(src, block, s_wy.at[a, j, k, d // 2], at(y=y + d))

    def quarter(parity, e):
        return pl.ds(pl.multiple_of(parity * 32 + e * 16, 16), 16)

    def far_push(a, j, k, d):
        for e in range(2):
            block = weights[a][j].at[side(k), (y + d) % 4, c, quarter(p, e)]
            push(block, block, s_wx.at[a, j, k, e, d], at(x=x + (1 if e == 0 else 3)))

    def far_f(a, j, k):
        for e in range(2):
            d = 1 if e == 0 else 3
            near = weights[a][j].at[side(k), (y + 4 - d) % 4, c]
            arrived(near.at[half], s_wy.at[a, j, k, e])
            push(near.at[quarter(p, e)], near.at[quarter(p, e)], s_wf.at[a, j, k, e], at(y=y + d))
        if k == 1:
            far_push(a, j, k, 0)
        far_push(a, j, k, 3)
        far_push(a, j, k, 1)

    def far_x(a, j, k):
        for e in range(2):
            arrived(weights[a][j].at[side(k), (y + 2) % 4, c, quarter(p, e)], s_wf.at[a, j, k, e])
        far_push(a, j, k, 2)
        if k == 0:
            own_copies[a][j].wait()
        block = weights[a][j].at[side(k), :, c, half]
        push(block, block, s_wd.at[a, j, k, 0], at(c=1 - c))

    def far_d(a, j, k):
        for d in ((3, 1, 2) if k == 0 else (0, 3, 1, 2)):
            for e in range(2):
                arrived(weights[a][j].at[side(k), (y + d) % 4, c, quarter(1 - p, e)], s_wx.at[a, j, k, e, d])
        block = weights[a][j].at[side(k), :, c, other_half]
        push(block, block, s_wd.at[a, j, k, 1], at(c=1 - c))

    def near_z(j):
        push(weights_in[0][j].at[half], weights[0][j].at[h, y, c, half], s_wz.at[0, j], at(z=7 - z))

    def near_y(j, k):
        block = weights[0][j].at[side(k), y, c, half]
        if k == 1:
            arrived(block, s_wz.at[0, j])
        src = weights_in[0][j].at[half] if k == 0 else block
        for d in (1, 3, 2):
            push(src, block, s_ny.at[j, k, d - 1], at(y=y + d))

    def near_x(j, k):
        if k == 0:
            own_copies[0][j].wait()
        for d in (1, 3, 2):
            arrived(weights[0][j].at[side(k), (y + 4 - d) % 4, c, half], s_ny.at[j, k, d - 1])
        for e in range(2):
            block = weights[0][j].at[side(k), :, c, quarter(p, e)]
            push(block, block, s_wx.at[0, j, k, e, 0], at(x=x + (1 if e == 0 else 3)))
        block = weights[0][j].at[side(k), :, c, half]
        push(block, block, s_wd.at[0, j, k, 0], at(c=1 - c))

    def near_d(j, k):
        for e in range(2):
            arrived(weights[0][j].at[side(k), :, c, quarter(1 - p, e)], s_wx.at[0, j, k, e, 0])
        block = weights[0][j].at[side(k), :, c, other_half]
        push(block, block, s_wd.at[0, j, k, 1], at(c=1 - c))

    def weights_ready(a, j):
        for k in range(2):
            arrived(weights[a][j].at[side(k), :, 1 - c, half], s_wd.at[a, j, k, 0])
            arrived(weights[a][j].at[side(k), :, 1 - c, other_half], s_wd.at[a, j, k, 1])

    mine = jnp.logical_or(owners[0] == lead, owners[1] == lead)
    keep = jnp.where(mine, 1.0, 0.0).astype(F32)

    def reduce_x(b):
        for d in (1, 3, 2):
            xt = (x + d) % 4
            push(slab.at[xt, :, b], rx.at[d - 1, :, b], s_rx.at[b, d - 1], at(x=xt))

    def reduce_x_arrived(b):
        for d in (1, 3, 2):
            arrived(rx.at[d - 1, :, b], s_rx.at[b, d - 1])

    def reduce_z(b):
        for i in range(4):
            total = slab[x, i, b].astype(F32) + rx[0, i, b].astype(F32)
            total = total + rx[1, i, b].astype(F32) + rx[2, i, b].astype(F32)
            sx[i, b] = total.astype(BF)
        for d in (1, 3, 2):
            zt = (zl + d) % 4
            push(sx.at[zt, b], rz.at[d - 1, b], s_rz.at[b, d - 1], at(z=h * 4 + zt))

    def gather_x(b):
        for d in (1, 3, 2):
            arrived(rz.at[d - 1, b], s_rz.at[b, d - 1])
        total = sx[zl, b].astype(F32) + rz[0, b].astype(F32) + rz[1, b].astype(F32) + rz[2, b].astype(F32)
        total = total * lax.rsqrt(jnp.mean(total * total, axis=-1, keepdims=True) + 1e-06)
        nb[h, x, zl, b] = total.astype(BF)
        piece = nb.at[h, x, zl, b]
        for d in (1, 3, 2):
            push(piece, piece, s_ax.at[b, d - 1], at(x=x + d))

    def gather_x_arrived(b):
        for d in (1, 3, 2):
            arrived(nb.at[h, (x + 4 - d) % 4, zl, b], s_ax.at[b, d - 1])

    def ring_piece(source, t, way, b):
        rows = pl.ds(0, 4) if t < 4 else pl.ds(2 * way, 2)
        return nb.at[source // 4, rows, source % 4, b]

    def ring_send(t, b):
        for way in range(2):
            source = zmod(z - (t - 1)) if way == 0 else zmod(z + (t - 1))
            target = zmod(z + 1) if way == 0 else zmod(z - 1)
            piece = ring_piece(source, t, way, b)
            push(piece, piece, s_az.at[b, t - 1, way], at(z=target))

    def ring_arrived(t, b):
        for way in range(2):
            source = zmod(z - t) if way == 0 else zmod(z + t)
            arrived(ring_piece(source, t, way, b), s_az.at[b, t - 1, way])

    near_z(0)
    near_y(0, 0)
    slab_copy.wait()

    @pl.loop(0, 16)
    def _(i):
        slab[i // 4, i % 4] = (slab[i // 4, i % 4].astype(F32) * keep).astype(BF)

    reduce_x(0)
    near_z(1)
    reduce_x_arrived(0)
    reduce_x(1)
    reduce_z(0)
    near_y(0, 1)
    gather_x(0)
    near_y(1, 0)
    near_x(0, 0)
    reduce_x_arrived(1)
    reduce_z(1)
    gather_x_arrived(0)
    ring_send(1, 0)
    gather_x(1)
    near_x(0, 1)
    near_y(1, 1)
    ring_arrived(1, 0)
    ring_send(2, 0)
    gather_x_arrived(1)
    ring_send(1, 1)
    near_x(1, 0)
    far_y(1, 0, 0)
    far_z(1, 0)
    ring_arrived(2, 0)
    ring_send(3, 0)
    ring_arrived(1, 1)
    ring_send(2, 1)
    near_x(1, 1)
    near_d(0, 0)
    ring_arrived(3, 0)
    ring_send(4, 0)
    ring_arrived(2, 1)
    ring_send(3, 1)
    near_d(0, 1)
    far_f(1, 0, 0)
    far_z(1, 1)
    far_y(1, 1, 0)
    ring_arrived(4, 0)
    ring_arrived(3, 1)
    ring_send(4, 1)
    near_d(1, 0)
    near_d(1, 1)
    far_x(1, 0, 0)
    far_y(1, 0, 1)
    far_f(1, 1, 0)
    far_y(1, 1, 1)
    for copy in table_copies:
        copy.wait()
    time = lead_ids[0]
    film_gain = 1.0 + scale_t[pl.ds(time, 1), :]
    film_bias = shift_t[pl.ds(time, 1), :]
    ring_arrived(4, 1)
    weights_ready(0, 0)

    def row_step(hp, first, second):
        @pl.loop(0, 8)
        def _(i):
            part = nb[hp, i // 2, pl.ds((i % 2) * 2, 2)].reshape(64, C)
            rows = pl.ds(pl.multiple_of(i * 64, 64), 64)
            hid[rows, :] = (part.astype(F32) * film_gain + film_bias).astype(BF)

        @pl.loop(0, 2)
        def _(t):
            block = wqr[:, :, :, :, pl.ds(pl.multiple_of(C + t * TILE, TILE), TILE)].reshape(C, TILE)
            cut = pl.ds(pl.multiple_of(t * TILE, TILE), TILE)
            kv[:, cut] = jnp.dot(hid[...], block, preferred_element_type=F32).astype(BF)

        here = pl.ds(pl.multiple_of(h * 64, 64), 64)

        def wanted(cols_cut):
            return jnp.concatenate(
                [hid[pl.ds(pl.multiple_of(r * 128 + h * 64, 64), 64), cols_cut] for r in range(4)], axis=0
            )

        @pl.loop(0, 1)
        def _(t):
            cut = pl.ds(pl.multiple_of(t * TILE, TILE), TILE)
            block = wqr[:, :, :, :, cut].reshape(C, TILE)
            qb[:, cut] = jnp.dot(wanted(slice(None)), block, preferred_element_type=F32).astype(BF)

        first()

        for head in range(HEADS):
            cut = slice(head * DIM, (head + 1) * DIM)
            vcut = slice(C + head * DIM, C + (head + 1) * DIM)
            q = qb[:, cut].reshape(4, 64, DIM)
            keys = kv[:, cut].reshape(4, 128, DIM)
            values = kv[:, vcut].reshape(4, 128, DIM)
            scores = lax.dot_general(q, keys, (((2,), (2,)), ((0,), (0,))), preferred_element_type=F32)
            probs = softmax_rows(scores).astype(BF)
            mix = lax.dot_general(probs, values, (((2,), (1,)), ((0,), (0,))), preferred_element_type=F32)
            mixed[pl.ds(0, 256), cut] = mix.reshape(256, DIM).astype(BF)

        second()

        @pl.loop(0, 1)
        def _(t):
            cut = pl.ds(pl.multiple_of(t * TILE, TILE), TILE)
            block = wor[:, :, :, :, cut].reshape(C, TILE)
            grown = jnp.dot(mixed[pl.ds(0, 256), :], block, preferred_element_type=F32)
            grown = (grown + wanted(cut).astype(F32)).reshape(4, 64, TILE)
            for d in range(8):
                send[hp, d, :, cut] = grown[:, d * 8 : (d + 1) * 8, :].reshape(32, TILE).astype(BF)

        for dy in (2, 1, 3, 0):
            for dc in range(2):
                if dy == 0 and dc == 0:
                    continue
                ty, tc = (y + dy) % 4, (c + dc) % 2
                push(
                    send.at[hp, ty * 2 + tc], cols.at[hp, yc], s_a2a.at[hp, dy * 2 + dc], at(y=ty, c=tc)
                )
        return pull(send.at[hp, yc], cols.at[hp, yc])

    def row_arrived(hp):
        for dy in (2, 1, 3, 0):
            for dc in range(2):
                if dy == 0 and dc == 0:
                    continue
                sy, sc = (y + 4 - dy) % 4, (c + dc) % 2
                arrived(cols.at[hp, sy * 2 + sc], s_a2a.at[hp, dy * 2 + dc])

    def after_first_projection():
        far_f(1, 0, 1)
        far_x(1, 1, 0)
        far_d(1, 0, 0)

    def after_first_mix():
        far_f(1, 1, 1)
        far_x(1, 0, 1)
        weights_ready(0, 1)

    def after_second_projection():
        far_x(1, 1, 1)
        far_d(1, 1, 0)
        far_d(1, 0, 1)

    def after_second_mix():
        far_d(1, 1, 1)

    own0 = row_step(0, after_first_projection, after_first_mix)
    own1 = row_step(1, after_second_projection, after_second_mix)
    own0.wait()
    own1.wait()
    row_arrived(0)
    row_arrived(1)

    for hp in range(2):
        @pl.loop(0, 8)
        def _(i):
            part = cols[hp, i].astype(F32)
            part = part * lax.rsqrt(jnp.mean(part * part, axis=-1, keepdims=True) + 1e-06) * gain[...]
            rows = pl.ds(pl.multiple_of(hp * 256 + i * 32, 32), 32)
            for s in range(8):
                xf[s, rows, :] = part[:, s * DIM : (s + 1) * DIM]

    for w in range(8):
        for s in range(8):
            hid[w * 64 : (w + 1) * 64, s * DIM : (s + 1) * DIM] = xf[s, pl.ds(w, 64, stride=8), :].astype(BF)

    weights_ready(1, 0)

    @pl.loop(0, 2)
    def _(t):
        block = wqc[:, :, :, :, pl.ds(pl.multiple_of(C + t * TILE, TILE), TILE)].reshape(C, TILE)
        cut = pl.ds(pl.multiple_of(t * TILE, TILE), TILE)
        kv[:, cut] = jnp.dot(hid[...], block, preferred_element_type=F32).astype(BF)

    @pl.loop(0, 1)
    def _(t):
        cut = pl.ds(pl.multiple_of(t * TILE, TILE), TILE)
        block = wqc[:, :, :, :, cut].reshape(C, TILE)
        mixed[:, cut] = jnp.dot(hid[...], block, preferred_element_type=F32).astype(BF)

    for head in range(HEADS):
        cut = slice(head * DIM, (head + 1) * DIM)
        vcut = slice(C + head * DIM, C + (head + 1) * DIM)
        q = mixed[:, cut].reshape(8, 64, DIM)
        keys = kv[:, cut].reshape(8, 64, DIM)
        values = kv[:, vcut].reshape(8, 64, DIM)
        scores = lax.dot_general(q, keys, (((2,), (2,)), ((0,), (0,))), preferred_element_type=F32)
        probs = softmax_rows(scores).astype(BF)
        mix = lax.dot_general(probs, values, (((2,), (1,)), ((0,), (0,))), preferred_element_type=F32)
        for w in range(8):
            xf[head, pl.ds(w, 64, stride=8), :] = mix[w]
        hid[:, cut] = xf[head].astype(BF)

    weights_ready(1, 1)

    @pl.loop(0, 1)
    def _(t):
        cut = pl.ds(pl.multiple_of(t * TILE, TILE), TILE)
        block = woc[:, :, :, :, cut].reshape(C, TILE)
        grown = jnp.dot(hid[...], block, preferred_element_type=F32)
        out[:, cut] = (grown + cols[:, :, :, cut].reshape(512, TILE).astype(F32)).astype(BF)

    for copy in started:
        copy.wait_send()

    @pl.when(edge)
    def _():
        for a in range(1, 2):
            for j in range(2):
                for forward in (False, True):
                    edge_copy(a, j, forward).wait_send()


def on_device(
    latents, owners, lead_ids, film_scale, film_shift, w_qkv_row, w_out_row, gain_col, w_qkv_col, w_out_col
):
    anywhere = pl.BlockSpec(memory_space=pl.ANY)
    scalars = pl.BlockSpec(memory_space=pltpu.SMEM)
    vector = pl.BlockSpec(memory_space=pltpu.VMEM)
    dma = pltpu.SemaphoreType.DMA
    result = pl.pallas_call(
        kernel,
        out_shape=jax.ShapeDtypeStruct((512, C), BF),
        in_specs=[
            anywhere, scalars, scalars, anywhere, anywhere, anywhere, anywhere, vector, anywhere, anywhere
        ],
        out_specs=vector,
        scratch_shapes=[
            pltpu.VMEM((4, 4, 2, 16, C), BF),
            pltpu.VMEM((360, C), F32),
            pltpu.VMEM((360, C), F32),
            pltpu.VMEM((3, 4, 2, 16, C), BF),
            pltpu.VMEM((4, 2, 16, C), BF),
            pltpu.VMEM((3, 2, 16, C), BF),
            pltpu.VMEM((2, 4, 4, 2, 16, C), BF),
            pltpu.VMEM((512, C), BF),
            pltpu.VMEM((512, 2 * C), BF),
            pltpu.VMEM((256, C), BF),
            pltpu.VMEM((512, C), BF),
            pltpu.VMEM((2, 8, 32, C), BF),
            pltpu.VMEM((2, 8, 32, C), BF),
            pltpu.VMEM((8, 512, DIM), F32),
            pltpu.VMEM((2, 4, 2, 64, 3 * C), BF),
            pltpu.VMEM((2, 4, 2, 64, C), BF),
            pltpu.VMEM((2, 4, 2, 64, 3 * C), BF),
            pltpu.VMEM((2, 4, 2, 64, C), BF),
            dma((SENDS,)),
            dma((9,)),
            dma((2, 3)),
            dma((2, 3)),
            dma((2, 3)),
            dma((2, 4, 2)),
            dma((2, 2, 2)),
            dma((2, 2, 3)),
            dma((2, 2)),
            dma((2, 2, 2, 2)),
            dma((2, 2, 2, 2)),
            dma((2, 2, 2, 2, 4)),
            dma((2, 2, 2, 2)),
            dma((2, 8)),
        ],
        compiler_params=pltpu.CompilerParams(
            collective_id=0, has_side_effects=True, vmem_limit_bytes=56 << 20
        ),
        name="axial_attention",
    )(
        latents.reshape(4, 4, 2, 16, C), owners, lead_ids, film_scale, film_shift,
        w_qkv_row, w_out_row, gain_col.reshape(1, C), w_qkv_col, w_out_col,
    )
    return result.reshape(1, 64, 8, C)


def solution(mesh):
    placed = (
        P("lead", "space", None, None),
        P(),
        P("lead"),
        P(),
        P(),
        P("space", None),
        P("space", None),
        P(),
        P("space", None),
        P("space", None),
    )
    return jax.shard_map(
        on_device,
        mesh=mesh,
        in_specs=placed,
        out_specs=P("lead", None, "space", None),
        check_vma=False,
    )
```

time: 124 us -> 107 us (0.86); the launches traced: 124 us -> 105 us
  Pallas kernels: 121 us -> 102 us
    pallas_call x1, Pallas kernels: 121 us -> 102 us  [on_device(): pl.pallas_call(kernel, out_shape=jax.ShapeDtypeStruct((512, C), BF), in_s...]
where the time goes in v2:
time: 107 us; the launch traced here: 105 us
  Pallas kernels  102 us (95%)
  local copies, waits for them, and re-layouts  2.26 us (2%)
    pallas_call x1, Pallas kernels, on_device(): pl.pallas_call(kernel, out_shape=jax.ShapeDtypeStruct((512, C), BF), in_s...  102 us
    unnamed x1, local copies, waits for them, and re-layouts  2.26 us

profile of v2, /device:TPU:1, one launch (start us, length us, event | category | flops | bytes accessed | tf_op | source)
XLA Modules:
  0.0 104.6 jit_solution(8584676358126666435)
XLA Ops:
  0.7 101.7 %axial_attention.1 = bf16[512,1024]{1,0:T(8,128)(2,1)} custom-call(bf16[4,4,2,16,1024]{4,3,2,1,0:T(8,128)(2,1)} %bitcast.4, s32[2]{0:T(128)} %owners.1, s32[1]{0:T(128)S(6)} %copy.12.lead_ids, f32[360,1024]{1,0:T(8,128)} %scale_in.1, f32[360,1024]{1,0:T(8,128)} %shift_in.1, bf16[64,3072]{1,0:T(8,128)(2,1)} %wqr_in.1, bf16[64,1024]{1,0:T(8,128)(2,1)} %wor_in.1, ...), custom_call_target="tpu_custom_call" | custom-call | tf_op jit(solution)/shard_map/axial_attention/pallas_call | solution.py:468
  102.3 2.3 %copy.13 = bf16[1,64,8,1024]{3,2,1,0:T(8,128)(2,1)} copy(bf16[1,64,8,1024]{3,2,1,0:T(8,128)(2,1)} %bitcast.3) | data formatting | bytes 2097152

commit v3 on v2

--- a/solution.py
+++ b/solution.py
@@ -17,16 +17,21 @@
 SENDS = 200
 
 
-def softmax_rows(scores):
+def attend(q, keys, values):
+    batch, count, _ = q.shape
+    scores = lax.dot_general(q, keys, (((2,), (2,)), ((0,), (0,))), preferred_element_type=F32)
     top = jnp.max(scores, axis=-1, keepdims=True)
-    weights = jnp.exp((scores - top) * (DIM**-0.5))
-    return weights / jnp.sum(weights, axis=-1, keepdims=True)
+    weights = jnp.exp((scores - top) * (DIM**-0.5)).astype(BF)
+    mix = lax.dot_general(weights, values, (((2,), (1,)), ((0,), (0,))), preferred_element_type=F32)
+    ones = jnp.ones((keys.shape[1], DIM), BF)
+    total = jnp.dot(weights.reshape(batch * count, keys.shape[1]), ones, preferred_element_type=F32)
+    return mix.reshape(batch * count, DIM) / total
 
 
 def kernel(
     slab_in, owners, lead_ids, scale_in, shift_in, wqr_in, wor_in, gain, wqc_in, woc_in,
     out,
-    slab, scale_t, shift_t, rx, sx, rz, nb, hid, kv, qb, mixed, send, cols, xf,
+    slab, scale_t, shift_t, rx, sx, rz, nb, hid, xt, kv, kvc, qb, mixed, send, cols, xf,
     wqr, wor, wqc, woc,
     ssem, loc, s_rx, s_rz, s_ax, s_az, s_edge, s_ny, s_wz, s_wy, s_wf, s_wx, s_wd, s_a2a,
 ):
@@ -85,6 +90,14 @@
     peers += [at(z=7 - z), at(c=1 - c)]
     for peer in peers:
         pl.semaphore_signal(barrier, 1, device_id=peer, device_id_type=MESH)
+    mine = jnp.logical_or(owners[0] == lead, owners[1] == lead)
+    keep = jnp.where(mine, 1.0, 0.0).astype(F32)
+    slab_copy.wait()
+
+    @pl.loop(0, 16)
+    def _(i):
+        slab[i // 4, i % 4] = (slab[i // 4, i % 4].astype(F32) * keep).astype(BF)
+
     pl.semaphore_wait(barrier, len(peers))
 
     def side(k):
@@ -106,21 +119,29 @@
             device_id_type=MESH,
         )
 
-    def far_z(a, j):
+    def mirror_send(a, j):
         @pl.when(edge)
         def _():
             edge_copy(a, j, False).start()
 
+    def mirror_pass(a, j):
+        @pl.when(edge)
+        def _():
+            arrived(weights[a][j].at[1 - h, y, c, half], s_wz.at[a, j])
+            edge_copy(a, j, True).start()
+
+    def mirror_wait(a, j):
+        @pl.when(jnp.logical_not(edge))
+        def _():
+            arrived(weights[a][j].at[1 - h, y, c, half], s_wz.at[a, j])
+
     def far_y(a, j, k):
-        block = weights[a][j].at[side(k), y, c, half]
+        block = weights[a][j].at[side(k), y, c]
+        src = weights_in[a][j]
         if k == 1:
-            arrived(block, s_wz.at[a, j])
-
-            @pl.when(edge)
-            def _():
-                edge_copy(a, j, True).start()
-
-        src = weights_in[a][j].at[half] if k == 0 else block
+            block = block.at[half]
+            src = block
+            mirror_wait(a, j)
         for d in (1, 3):
             push(src, block, s_wy.at[a, j, k, d // 2], at(y=y + d))
 
@@ -132,40 +153,42 @@
             block = weights[a][j].at[side(k), (y + d) % 4, c, quarter(p, e)]
             push(block, block, s_wx.at[a, j, k, e, d], at(x=x + (1 if e == 0 else 3)))
 
+    def passed_on(k, e):
+        return quarter(p, e) if k == 1 else pl.ds(e * 32, 32)
+
     def far_f(a, j, k):
         for e in range(2):
             d = 1 if e == 0 else 3
             near = weights[a][j].at[side(k), (y + 4 - d) % 4, c]
-            arrived(near.at[half], s_wy.at[a, j, k, e])
-            push(near.at[quarter(p, e)], near.at[quarter(p, e)], s_wf.at[a, j, k, e], at(y=y + d))
+            arrived(near.at[half] if k == 1 else near, s_wy.at[a, j, k, e])
+            piece = near.at[passed_on(k, e)]
+            push(piece, piece, s_wf.at[a, j, k, e], at(y=y + d))
         if k == 1:
-            far_push(a, j, k, 0)
-        far_push(a, j, k, 3)
-        far_push(a, j, k, 1)
+            for d in (0, 3, 1):
+                far_push(a, j, k, d)
 
     def far_x(a, j, k):
         for e in range(2):
-            arrived(weights[a][j].at[side(k), (y + 2) % 4, c, quarter(p, e)], s_wf.at[a, j, k, e])
-        far_push(a, j, k, 2)
+            arrived(weights[a][j].at[side(k), (y + 2) % 4, c, passed_on(k, e)], s_wf.at[a, j, k, e])
+        block = weights[a][j].at[side(k), :, c]
         if k == 0:
             own_copies[a][j].wait()
-        block = weights[a][j].at[side(k), :, c, half]
+        else:
+            far_push(a, j, k, 2)
+            block = weights[a][j].at[side(k), :, c, half]
         push(block, block, s_wd.at[a, j, k, 0], at(c=1 - c))
 
-    def far_d(a, j, k):
-        for d in ((3, 1, 2) if k == 0 else (0, 3, 1, 2)):
+    def far_d(a, j):
+        for d in (0, 3, 1, 2):
             for e in range(2):
-                arrived(weights[a][j].at[side(k), (y + d) % 4, c, quarter(1 - p, e)], s_wx.at[a, j, k, e, d])
-        block = weights[a][j].at[side(k), :, c, other_half]
-        push(block, block, s_wd.at[a, j, k, 1], at(c=1 - c))
-
-    def near_z(j):
-        push(weights_in[0][j].at[half], weights[0][j].at[h, y, c, half], s_wz.at[0, j], at(z=7 - z))
+                arrived(weights[a][j].at[side(1), (y + d) % 4, c, quarter(1 - p, e)], s_wx.at[a, j, 1, e, d])
+        block = weights[a][j].at[side(1), :, c, other_half]
+        push(block, block, s_wd.at[a, j, 1, 1], at(c=1 - c))
 
     def near_y(j, k):
         block = weights[0][j].at[side(k), y, c, half]
         if k == 1:
-            arrived(block, s_wz.at[0, j])
+            mirror_wait(0, j)
         src = weights_in[0][j].at[half] if k == 0 else block
         for d in (1, 3, 2):
             push(src, block, s_ny.at[j, k, d - 1], at(y=y + d))
@@ -189,11 +212,12 @@
 
     def weights_ready(a, j):
         for k in range(2):
+            if a == 1 and k == 0:
+                arrived(weights[a][j].at[side(k), :, 1 - c], s_wd.at[a, j, k, 0])
+                continue
             arrived(weights[a][j].at[side(k), :, 1 - c, half], s_wd.at[a, j, k, 0])
             arrived(weights[a][j].at[side(k), :, 1 - c, other_half], s_wd.at[a, j, k, 1])
 
-    mine = jnp.logical_or(owners[0] == lead, owners[1] == lead)
-    keep = jnp.where(mine, 1.0, 0.0).astype(F32)
 
     def reduce_x(b):
         for d in (1, 3, 2):
@@ -243,117 +267,42 @@
             source = zmod(z - t) if way == 0 else zmod(z + t)
             arrived(ring_piece(source, t, way, b), s_az.at[b, t - 1, way])
 
-    near_z(0)
-    near_y(0, 0)
-    slab_copy.wait()
-
-    @pl.loop(0, 16)
-    def _(i):
-        slab[i // 4, i % 4] = (slab[i // 4, i % 4].astype(F32) * keep).astype(BF)
-
-    reduce_x(0)
-    near_z(1)
-    reduce_x_arrived(0)
-    reduce_x(1)
-    reduce_z(0)
-    near_y(0, 1)
-    gather_x(0)
-    near_y(1, 0)
-    near_x(0, 0)
-    reduce_x_arrived(1)
-    reduce_z(1)
-    gather_x_arrived(0)
-    ring_send(1, 0)
-    gather_x(1)
-    near_x(0, 1)
-    near_y(1, 1)
-    ring_arrived(1, 0)
-    ring_send(2, 0)
-    gather_x_arrived(1)
-    ring_send(1, 1)
-    near_x(1, 0)
-    far_y(1, 0, 0)
-    far_z(1, 0)
-    ring_arrived(2, 0)
-    ring_send(3, 0)
-    ring_arrived(1, 1)
-    ring_send(2, 1)
-    near_x(1, 1)
-    near_d(0, 0)
-    ring_arrived(3, 0)
-    ring_send(4, 0)
-    ring_arrived(2, 1)
-    ring_send(3, 1)
-    near_d(0, 1)
-    far_f(1, 0, 0)
-    far_z(1, 1)
-    far_y(1, 1, 0)
-    ring_arrived(4, 0)
-    ring_arrived(3, 1)
-    ring_send(4, 1)
-    near_d(1, 0)
-    near_d(1, 1)
-    far_x(1, 0, 0)
-    far_y(1, 0, 1)
-    far_f(1, 1, 0)
-    far_y(1, 1, 1)
-    for copy in table_copies:
-        copy.wait()
-    time = lead_ids[0]
-    film_gain = 1.0 + scale_t[pl.ds(time, 1), :]
-    film_bias = shift_t[pl.ds(time, 1), :]
-    ring_arrived(4, 1)
-    weights_ready(0, 0)
-
-    def row_step(hp, first, second):
+    here = pl.ds(pl.multiple_of(h * 2, 2), 2)
+
+    def project(b):
         @pl.loop(0, 8)
         def _(i):
-            part = nb[hp, i // 2, pl.ds((i % 2) * 2, 2)].reshape(64, C)
-            rows = pl.ds(pl.multiple_of(i * 64, 64), 64)
-            hid[rows, :] = (part.astype(F32) * film_gain + film_bias).astype(BF)
+            part = nb[i // 4, i % 4, :, b].reshape(64, C)
+            grown = (part.astype(F32) * film_gain + film_bias).astype(BF)
+            hid[i // 4, i % 4, :, b] = grown.reshape(4, 16, C)
 
         @pl.loop(0, 2)
         def _(t):
             block = wqr[:, :, :, :, pl.ds(pl.multiple_of(C + t * TILE, TILE), TILE)].reshape(C, TILE)
             cut = pl.ds(pl.multiple_of(t * TILE, TILE), TILE)
-            kv[:, cut] = jnp.dot(hid[...], block, preferred_element_type=F32).astype(BF)
-
-        here = pl.ds(pl.multiple_of(h * 64, 64), 64)
-
-        def wanted(cols_cut):
-            return jnp.concatenate(
-                [hid[pl.ds(pl.multiple_of(r * 128 + h * 64, 64), 64), cols_cut] for r in range(4)], axis=0
-            )
-
-        @pl.loop(0, 1)
-        def _(t):
-            cut = pl.ds(pl.multiple_of(t * TILE, TILE), TILE)
-            block = wqr[:, :, :, :, cut].reshape(C, TILE)
-            qb[:, cut] = jnp.dot(wanted(slice(None)), block, preferred_element_type=F32).astype(BF)
-
-        first()
-
+            tokens = hid[:, :, :, b].reshape(512, C)
+            grown = jnp.dot(tokens, block, preferred_element_type=F32).astype(BF)
+            kv[:, :, :, b, :, cut] = grown.reshape(2, 4, 4, 16, TILE)
+
+        block = wqr[:, :, :, :, :C].reshape(C, C)
+        tokens = hid[:, :, here, b].reshape(256, C)
+        grown = jnp.dot(tokens, block, preferred_element_type=F32).astype(BF)
+        qb[:, :, :, b] = grown.reshape(2, 4, 2, 16, C)
+
+    def row_step(hp):
         for head in range(HEADS):
             cut = slice(head * DIM, (head + 1) * DIM)
             vcut = slice(C + head * DIM, C + (head + 1) * DIM)
-            q = qb[:, cut].reshape(4, 64, DIM)
-            keys = kv[:, cut].reshape(4, 128, DIM)
-            values = kv[:, vcut].reshape(4, 128, DIM)
-            scores = lax.dot_general(q, keys, (((2,), (2,)), ((0,), (0,))), preferred_element_type=F32)
-            probs = softmax_rows(scores).astype(BF)
-            mix = lax.dot_general(probs, values, (((2,), (1,)), ((0,), (0,))), preferred_element_type=F32)
-            mixed[pl.ds(0, 256), cut] = mix.reshape(256, DIM).astype(BF)
-
-        second()
-
-        @pl.loop(0, 1)
-        def _(t):
-            cut = pl.ds(pl.multiple_of(t * TILE, TILE), TILE)
-            block = wor[:, :, :, :, cut].reshape(C, TILE)
-            grown = jnp.dot(mixed[pl.ds(0, 256), :], block, preferred_element_type=F32)
-            grown = (grown + wanted(cut).astype(F32)).reshape(4, 64, TILE)
-            for d in range(8):
-                send[hp, d, :, cut] = grown[:, d * 8 : (d + 1) * 8, :].reshape(32, TILE).astype(BF)
+            q = qb[hp, :, :, :, :, cut].reshape(4, 64, DIM)
+            keys = kv[hp, :, :, :, :, cut].reshape(4, 128, DIM)
+            values = kv[hp, :, :, :, :, vcut].reshape(4, 128, DIM)
+            mixed[pl.ds(0, 256), cut] = attend(q, keys, values).astype(BF)
+
+        block = wor[...].reshape(C, C)
+        grown = jnp.dot(mixed[pl.ds(0, 256), :], block, preferred_element_type=F32)
+        grown = (grown + hid[hp, :, here].reshape(256, C).astype(F32)).reshape(4, 64, C)
+        for d in range(8):
+            send[hp, d] = grown[:, d * 8 : (d + 1) * 8, :].reshape(32, C).astype(BF)
 
         for dy in (2, 1, 3, 0):
             for dc in range(2):
@@ -373,32 +322,78 @@
                 sy, sc = (y + 4 - dy) % 4, (c + dc) % 2
                 arrived(cols.at[hp, sy * 2 + sc], s_a2a.at[hp, dy * 2 + dc])
 
-    def after_first_projection():
-        far_f(1, 0, 1)
-        far_x(1, 1, 0)
-        far_d(1, 0, 0)
-
-    def after_first_mix():
-        far_f(1, 1, 1)
-        far_x(1, 0, 1)
-        weights_ready(0, 1)
-
-    def after_second_projection():
-        far_x(1, 1, 1)
-        far_d(1, 1, 0)
-        far_d(1, 0, 1)
-
-    def after_second_mix():
-        far_d(1, 1, 1)
-
-    own0 = row_step(0, after_first_projection, after_first_mix)
-    own1 = row_step(1, after_second_projection, after_second_mix)
-    own0.wait()
-    own1.wait()
-    row_arrived(0)
-    row_arrived(1)
-
-    for hp in range(2):
+    reduce_x(0)
+    mirror_send(0, 0)
+    near_y(0, 0)
+    mirror_send(0, 1)
+    mirror_pass(0, 0)
+    reduce_x_arrived(0)
+    reduce_x(1)
+    reduce_z(0)
+    mirror_pass(0, 1)
+    mirror_send(1, 0)
+    mirror_send(1, 1)
+    gather_x(0)
+    near_y(0, 1)
+    near_y(1, 0)
+    near_x(0, 0)
+    reduce_x_arrived(1)
+    reduce_z(1)
+    gather_x_arrived(0)
+    ring_send(1, 0)
+    mirror_pass(1, 0)
+    mirror_pass(1, 1)
+    gather_x(1)
+    near_y(1, 1)
+    near_x(0, 1)
+    ring_arrived(1, 0)
+    ring_send(2, 0)
+    gather_x_arrived(1)
+    ring_send(1, 1)
+    far_y(1, 0, 0)
+    near_x(1, 0)
+    ring_arrived(2, 0)
+    ring_send(3, 0)
+    ring_arrived(1, 1)
+    ring_send(2, 1)
+    near_x(1, 1)
+    near_d(0, 0)
+    far_y(1, 0, 1)
+    ring_arrived(3, 0)
+    ring_send(4, 0)
+    ring_arrived(2, 1)
+    ring_send(3, 1)
+    near_d(0, 1)
+    far_f(1, 0, 0)
+    far_y(1, 1, 0)
+    far_y(1, 1, 1)
+    ring_arrived(4, 0)
+    ring_arrived(3, 1)
+    ring_send(4, 1)
+    near_d(1, 0)
+    near_d(1, 1)
+    far_f(1, 0, 1)
+    for copy in table_copies:
+        copy.wait()
+    time = lead_ids[0]
+    film_gain = 1.0 + scale_t[pl.ds(time, 1), :]
+    film_bias = shift_t[pl.ds(time, 1), :]
+    weights_ready(0, 0)
+    project(0)
+    far_x(1, 0, 0)
+    far_x(1, 0, 1)
+    far_f(1, 1, 0)
+    far_f(1, 1, 1)
+    ring_arrived(4, 1)
+    project(1)
+    far_x(1, 1, 0)
+    far_x(1, 1, 1)
+    far_d(1, 0)
+    weights_ready(0, 1)
+    own0 = row_step(0)
+    far_d(1, 1)
+    own1 = row_step(1)
+    def prepare(hp):
         @pl.loop(0, 8)
         def _(i):
             part = cols[hp, i].astype(F32)
@@ -407,52 +402,47 @@
             for s in range(8):
                 xf[s, rows, :] = part[:, s * DIM : (s + 1) * DIM]
 
-    for w in range(8):
-        for s in range(8):
-            hid[w * 64 : (w + 1) * 64, s * DIM : (s + 1) * DIM] = xf[s, pl.ds(w, 64, stride=8), :].astype(BF)
-
+        for w in range(8):
+            for s in range(8):
+                taken = xf[s, pl.ds(hp * 256 + w, 32, stride=8), :]
+                xt[hp, w * 32 : (w + 1) * 32, s * DIM : (s + 1) * DIM] = taken.astype(BF)
+
+        @pl.loop(0, 3)
+        def _(t):
+            cut = pl.ds(pl.multiple_of(t * TILE, TILE), TILE)
+            block = wqc[:, :, :, :, cut].reshape(C, TILE)
+            grown = jnp.dot(xt[hp], block, preferred_element_type=F32).astype(BF)
+            kvc[:, hp, :, cut] = grown.reshape(8, 32, TILE)
+
+    own0.wait()
+    row_arrived(0)
     weights_ready(1, 0)
-
-    @pl.loop(0, 2)
-    def _(t):
-        block = wqc[:, :, :, :, pl.ds(pl.multiple_of(C + t * TILE, TILE), TILE)].reshape(C, TILE)
-        cut = pl.ds(pl.multiple_of(t * TILE, TILE), TILE)
-        kv[:, cut] = jnp.dot(hid[...], block, preferred_element_type=F32).astype(BF)
-
-    @pl.loop(0, 1)
-    def _(t):
-        cut = pl.ds(pl.multiple_of(t * TILE, TILE), TILE)
-        block = wqc[:, :, :, :, cut].reshape(C, TILE)
-        mixed[:, cut] = jnp.dot(hid[...], block, preferred_element_type=F32).astype(BF)
+    prepare(0)
+    own1.wait()
+    row_arrived(1)
+    prepare(1)
 
     for head in range(HEADS):
         cut = slice(head * DIM, (head + 1) * DIM)
-        vcut = slice(C + head * DIM, C + (head + 1) * DIM)
-        q = mixed[:, cut].reshape(8, 64, DIM)
-        keys = kv[:, cut].reshape(8, 64, DIM)
-        values = kv[:, vcut].reshape(8, 64, DIM)
-        scores = lax.dot_general(q, keys, (((2,), (2,)), ((0,), (0,))), preferred_element_type=F32)
-        probs = softmax_rows(scores).astype(BF)
-        mix = lax.dot_general(probs, values, (((2,), (1,)), ((0,), (0,))), preferred_element_type=F32)
+        q, keys, values = (
+            kvc[:, :, :, i * C + head * DIM : i * C + (head + 1) * DIM].reshape(8, 64, DIM) for i in range(3)
+        )
+        mix = attend(q, keys, values)
         for w in range(8):
-            xf[head, pl.ds(w, 64, stride=8), :] = mix[w]
-        hid[:, cut] = xf[head].astype(BF)
+            xf[head, pl.ds(w, 64, stride=8), :] = mix[w * 64 : (w + 1) * 64]
+        mixed[:, cut] = xf[head].astype(BF)
 
     weights_ready(1, 1)
-
-    @pl.loop(0, 1)
-    def _(t):
-        cut = pl.ds(pl.multiple_of(t * TILE, TILE), TILE)
-        block = woc[:, :, :, :, cut].reshape(C, TILE)
-        grown = jnp.dot(hid[...], block, preferred_element_type=F32)
-        out[:, cut] = (grown + cols[:, :, :, cut].reshape(512, TILE).astype(F32)).astype(BF)
+    block = woc[...].reshape(C, C)
+    grown = jnp.dot(mixed[...], block, preferred_element_type=F32)
+    out[...] = (grown + cols[...].reshape(512, C).astype(F32)).astype(BF)
 
     for copy in started:
         copy.wait_send()
 
     @pl.when(edge)
     def _():
-        for a in range(1, 2):
+        for a in range(2):
             for j in range(2):
                 for forward in (False, True):
                     edge_copy(a, j, forward).wait_send()
@@ -480,9 +470,11 @@
             pltpu.VMEM((4, 2, 16, C), BF),
             pltpu.VMEM((3, 2, 16, C), BF),
             pltpu.VMEM((2, 4, 4, 2, 16, C), BF),
-            pltpu.VMEM((512, C), BF),
-            pltpu.VMEM((512, 2 * C), BF),
-            pltpu.VMEM((256, C), BF),
+            pltpu.VMEM((2, 4, 4, 2, 16, C), BF),
+            pltpu.VMEM((2, 256, C), BF),
+            pltpu.VMEM((2, 4, 4, 2, 16, 2 * C), BF),
+            pltpu.VMEM((8, 2, 32, 3 * C), BF),
+            pltpu.VMEM((2, 4, 2, 2, 16, C), BF),
             pltpu.VMEM((512, C), BF),
             pltpu.VMEM((2, 8, 32, C), BF),
             pltpu.VMEM((2, 8, 32, C), BF),

time: 107 us -> 95.1 us (0.89); the launches traced: 105 us -> 95 us
  Pallas kernels: 102 us -> 92.1 us
    pallas_call x1, Pallas kernels: 102 us -> 92.1 us  [on_device(): pl.pallas_call(kernel, out_shape=jax.ShapeDtypeStruct((512, C), BF), in_s...]
where the time goes in v3:
time: 95.1 us; the launch traced here: 95 us
  Pallas kernels  92.1 us (97%)
  local copies, waits for them, and re-layouts  2.26 us (2%)
    pallas_call x1, Pallas kernels, on_device(): pl.pallas_call(kernel, out_shape=jax.ShapeDtypeStruct((512, C), BF), in_s...  92.1 us
    unnamed x1, local copies, waits for them, and re-layouts  2.26 us

profile of v3, /device:TPU:1, one launch (start us, length us, event | category | flops | bytes accessed | tf_op | source)
XLA Modules:
  0.0 95.0 jit_solution(17608923032000618572)
XLA Ops:
  0.7 92.1 %axial_attention.1 = bf16[512,1024]{1,0:T(8,128)(2,1)} custom-call(bf16[4,4,2,16,1024]{4,3,2,1,0:T(8,128)(2,1)} %bitcast.4, s32[2]{0:T(128)} %owners.1, s32[1]{0:T(128)S(6)} %copy.12.lead_ids, f32[360,1024]{1,0:T(8,128)} %scale_in.1, f32[360,1024]{1,0:T(8,128)} %shift_in.1, bf16[64,3072]{1,0:T(8,128)(2,1)} %wqr_in.1, bf16[64,1024]{1,0:T(8,128)(2,1)} %wor_in.1, ...), custom_call_target="tpu_custom_call" | custom-call | tf_op jit(solution)/shard_map/axial_attention/pallas_call | solution.py:458
  92.7 2.3 %copy.13 = bf16[1,64,8,1024]{3,2,1,0:T(8,128)(2,1)} copy(bf16[1,64,8,1024]{3,2,1,0:T(8,128)(2,1)} %bitcast.3) | data formatting | bytes 2097152

commit v4 on v3

--- a/solution.py
+++ b/solution.py
@@ -13,7 +13,6 @@
 MESH = pl.DeviceIdType.MESH
 BF = jnp.bfloat16
 F32 = jnp.float32
-TILE = 1024
 SENDS = 200
 
 
@@ -74,7 +73,7 @@
         local.append(copy)
         return copy
 
-    slab_copy = pull(slab_in, slab)
+    slab_copy = pull(slab_in.at[x], slab)
     half = pl.ds(pl.multiple_of(p * 32, 32), 32)
     other_half = pl.ds(pl.multiple_of((1 - p) * 32, 32), 32)
     own_copies = [
@@ -90,14 +89,6 @@
     peers += [at(z=7 - z), at(c=1 - c)]
     for peer in peers:
         pl.semaphore_signal(barrier, 1, device_id=peer, device_id_type=MESH)
-    mine = jnp.logical_or(owners[0] == lead, owners[1] == lead)
-    keep = jnp.where(mine, 1.0, 0.0).astype(F32)
-    slab_copy.wait()
-
-    @pl.loop(0, 16)
-    def _(i):
-        slab[i // 4, i % 4] = (slab[i // 4, i % 4].astype(F32) * keep).astype(BF)
-
     pl.semaphore_wait(barrier, len(peers))
 
     def side(k):
@@ -222,16 +213,21 @@
     def reduce_x(b):
         for d in (1, 3, 2):
             xt = (x + d) % 4
-            push(slab.at[xt, :, b], rx.at[d - 1, :, b], s_rx.at[b, d - 1], at(x=xt))
+            push(slab_in.at[xt, :, b], rx.at[d - 1, :, b], s_rx.at[b, d - 1], at(x=xt))
 
     def reduce_x_arrived(b):
         for d in (1, 3, 2):
             arrived(rx.at[d - 1, :, b], s_rx.at[b, d - 1])
+
+    def kept(d):
+        source = (x + 4 - d) % 4 * 4 + zl
+        return jnp.where(jnp.logical_or(owners[0] == source, owners[1] == source), 1.0, 0.0).astype(F32)
 
     def reduce_z(b):
         for i in range(4):
-            total = slab[x, i, b].astype(F32) + rx[0, i, b].astype(F32)
-            total = total + rx[1, i, b].astype(F32) + rx[2, i, b].astype(F32)
+            total = slab[i, b].astype(F32) * kept(0)
+            for d in range(1, 4):
+                total = total + rx[d - 1, i, b].astype(F32) * kept(d)
             sx[i, b] = total.astype(BF)
         for d in (1, 3, 2):
             zt = (zl + d) % 4
@@ -276,13 +272,9 @@
             grown = (part.astype(F32) * film_gain + film_bias).astype(BF)
             hid[i // 4, i % 4, :, b] = grown.reshape(4, 16, C)
 
-        @pl.loop(0, 2)
-        def _(t):
-            block = wqr[:, :, :, :, pl.ds(pl.multiple_of(C + t * TILE, TILE), TILE)].reshape(C, TILE)
-            cut = pl.ds(pl.multiple_of(t * TILE, TILE), TILE)
-            tokens = hid[:, :, :, b].reshape(512, C)
-            grown = jnp.dot(tokens, block, preferred_element_type=F32).astype(BF)
-            kv[:, :, :, b, :, cut] = grown.reshape(2, 4, 4, 16, TILE)
+        block = wqr[:, :, :, :, C:].reshape(C, 2 * C)
+        grown = jnp.dot(hid[:, :, :, b].reshape(512, C), block, preferred_element_type=F32).astype(BF)
+        kv[:, :, :, b] = grown.reshape(2, 4, 4, 16, 2 * C)
 
         block = wqr[:, :, :, :, :C].reshape(C, C)
         tokens = hid[:, :, here, b].reshape(256, C)
@@ -329,6 +321,7 @@
     mirror_pass(0, 0)
     reduce_x_arrived(0)
     reduce_x(1)
+    slab_copy.wait()
     reduce_z(0)
     mirror_pass(0, 1)
     mirror_send(1, 0)
@@ -407,12 +400,8 @@
                 taken = xf[s, pl.ds(hp * 256 + w, 32, stride=8), :]
                 xt[hp, w * 32 : (w + 1) * 32, s * DIM : (s + 1) * DIM] = taken.astype(BF)
 
-        @pl.loop(0, 3)
-        def _(t):
-            cut = pl.ds(pl.multiple_of(t * TILE, TILE), TILE)
-            block = wqc[:, :, :, :, cut].reshape(C, TILE)
-            grown = jnp.dot(xt[hp], block, preferred_element_type=F32).astype(BF)
-            kvc[:, hp, :, cut] = grown.reshape(8, 32, TILE)
+        grown = jnp.dot(xt[hp], wqc[...].reshape(C, 3 * C), preferred_element_type=F32).astype(BF)
+        kvc[:, hp] = grown.reshape(8, 32, 3 * C)
 
     own0.wait()
     row_arrived(0)
@@ -463,7 +452,7 @@
         ],
         out_specs=vector,
         scratch_shapes=[
-            pltpu.VMEM((4, 4, 2, 16, C), BF),
+            pltpu.VMEM((4, 2, 16, C), BF),
             pltpu.VMEM((360, C), F32),
             pltpu.VMEM((360, C), F32),
             pltpu.VMEM((3, 4, 2, 16, C), BF),

time: 95.1 us -> 94.4 us (level)
  no operation moved by 1% of the time
where the time goes in v4:
time: 94.4 us; the launch traced here: 94.3 us
  Pallas kernels  91.3 us (97%)
  local copies, waits for them, and re-layouts  2.26 us (2%)
    pallas_call x1, Pallas kernels, on_device(): pl.pallas_call(kernel, out_shape=jax.ShapeDtypeStruct((512, C), BF), in_s...  91.3 us
    unnamed x1, local copies, waits for them, and re-layouts  2.26 us

profile of v4, /device:TPU:1, one launch (start us, length us, event | category | flops | bytes accessed | tf_op | source)
XLA Modules:
  0.0 94.3 jit_solution(15768951369738363142)
XLA Ops:
  0.7 91.3 %axial_attention.1 = bf16[512,1024]{1,0:T(8,128)(2,1)} custom-call(bf16[4,4,2,16,1024]{4,3,2,1,0:T(8,128)(2,1)} %bitcast.4, s32[2]{0:T(128)} %owners.1, s32[1]{0:T(128)S(6)} %copy.12.lead_ids, f32[360,1024]{1,0:T(8,128)} %scale_in.1, f32[360,1024]{1,0:T(8,128)} %shift_in.1, bf16[64,3072]{1,0:T(8,128)(2,1)} %wqr_in.1, bf16[64,1024]{1,0:T(8,128)(2,1)} %wor_in.1, ...), custom_call_target="tpu_custom_call" | custom-call | tf_op jit(solution)/shard_map/axial_attention/pallas_call | solution.py:447
  92.0 2.3 %copy.13 = bf16[1,64,8,1024]{3,2,1,0:T(8,128)(2,1)} copy(bf16[1,64,8,1024]{3,2,1,0:T(8,128)(2,1)} %bitcast.3) | data formatting | bytes 2097152

commit v5 on v4

--- a/solution.py
+++ b/solution.py
@@ -30,7 +30,7 @@
 def kernel(
     slab_in, owners, lead_ids, scale_in, shift_in, wqr_in, wor_in, gain, wqc_in, woc_in,
     out,
-    slab, scale_t, shift_t, rx, sx, rz, nb, hid, xt, kv, kvc, qb, mixed, send, cols, xf,
+    stage, slab, scale_t, shift_t, rx, sx, rz, nb, hid, xt, kv, kvc, qb, mixed, send, cols, xf,
     wqr, wor, wqc, woc,
     ssem, loc, s_rx, s_rz, s_ax, s_az, s_edge, s_ny, s_wz, s_wy, s_wf, s_wx, s_wd, s_a2a,
 ):
@@ -423,8 +423,14 @@
 
     weights_ready(1, 1)
     block = woc[...].reshape(C, C)
-    grown = jnp.dot(mixed[...], block, preferred_element_type=F32)
-    out[...] = (grown + cols[...].reshape(512, C).astype(F32)).astype(BF)
+    written = []
+    for hp in range(2):
+        rows = pl.ds(hp * 256, 256)
+        grown = jnp.dot(mixed[rows, :], block, preferred_element_type=F32)
+        stage[rows, :] = (grown + cols[hp].reshape(256, C).astype(F32)).astype(BF)
+        written.append(pull(stage.at[rows], out.at[rows]))
+    for copy in written:
+        copy.wait()
 
     for copy in started:
         copy.wait_send()
@@ -450,8 +456,9 @@
         in_specs=[
             anywhere, scalars, scalars, anywhere, anywhere, anywhere, anywhere, vector, anywhere, anywhere
         ],
-        out_specs=vector,
+        out_specs=anywhere,
         scratch_shapes=[
+            pltpu.VMEM((512, C), BF),
             pltpu.VMEM((4, 2, 16, C), BF),
             pltpu.VMEM((360, C), F32),
             pltpu.VMEM((360, C), F32),
@@ -473,7 +480,7 @@
             pltpu.VMEM((2, 4, 2, 64, 3 * C), BF),
             pltpu.VMEM((2, 4, 2, 64, C), BF),
             dma((SENDS,)),
-            dma((9,)),
+            dma((11,)),
             dma((2, 3)),
             dma((2, 3)),
             dma((2, 3)),

time: 94.4 us -> 94.3 us (level)
  no operation moved by 1% of the time
where the time goes in v5:
time: 94.3 us; the launch traced here: 94.1 us
  Pallas kernels  91.2 us (97%)
  local copies, waits for them, and re-layouts  2.26 us (2%)
    pallas_call x1, Pallas kernels, on_device(): pl.pallas_call(kernel, out_shape=jax.ShapeDtypeStruct((512, C), BF), in_s...  91.2 us
    unnamed x1, local copies, waits for them, and re-layouts  2.26 us

profile of v5, /device:TPU:1, one launch (start us, length us, event | category | flops | bytes accessed | tf_op | source)
XLA Modules:
  0.0 94.1 jit_solution(7600160625176706849)
XLA Ops:
  0.7 91.2 %axial_attention.1 = bf16[512,1024]{1,0:T(8,128)(2,1)} custom-call(bf16[4,4,2,16,1024]{4,3,2,1,0:T(8,128)(2,1)} %bitcast.4, s32[2]{0:T(128)} %owners.1, s32[1]{0:T(128)S(6)} %copy.12.lead_ids, f32[360,1024]{1,0:T(8,128)} %scale_in.1, f32[360,1024]{1,0:T(8,128)} %shift_in.1, bf16[64,3072]{1,0:T(8,128)(2,1)} %wqr_in.1, bf16[64,1024]{1,0:T(8,128)(2,1)} %wor_in.1, ...), custom_call_target="tpu_custom_call" | custom-call | tf_op jit(solution)/shard_map/axial_attention/pallas_call | solution.py:453
  91.8 2.3 %copy.13 = bf16[1,64,8,1024]{3,2,1,0:T(8,128)(2,1)} copy(bf16[1,64,8,1024]{3,2,1,0:T(8,128)(2,1)} %bitcast.3) | data formatting | bytes 2097152
